TPU v7x, 128 devices: a whole 4x4x4 slice. The times are simulated.
128 devices in a mesh: sec: 8 (over x, core), op: 16 (over y, z).
Axes of the slice: x: 4, y: 4, z: 4, core: 2. Of those that a mesh axis runs over, the one named last changes fastest.
Arguments:
- psi: bfloat16 [8192, 256], P(('sec', 'op')), may hold values from -6 to 6
- left_env: bfloat16 [384, 32, 256, 256], P('op', 'sec'), may hold values from -0.01953125 to 0.01953125
- right_env: bfloat16 [384, 32, 256, 256], P('op', 'sec'), may hold values from -0.375 to 0.375
- term_src: int32 [384, 32], P('op', 'sec'), may hold values from 0 to 31, as said below
- block_dims: int32 [2, 32], replicated, may hold values from 64 to 256, as said below
Outputs:
- sigma: bfloat16 [8192, 256], P(('sec', 'op'))
Inputs may be any that keep to these rules, and one draw needn't show every extreme that they name: |term_src[t, k] - k| <= 2 for every t and k, and term_src[t, k] = k + 2 for some t and k. `block_dims`: every entry is a multiple of 4; 256 is reached in each row.
All inputs are finite; a program needn't handle non-finite values.
Results may differ from a plain program's by a relative error of at most 0.0049.
Values may be sent and summed in bfloat16 or wider, within the bound.
A program may use at most 128 MiB of HBM per device.

v0:
```python
import jax
import jax.numpy as jnp
from jax import lax
from jax.sharding import PartitionSpec as P


def padded(cells, sides, width):
    for axis, dim in sides:
        count = lax.axis_size(axis)
        ends = count - 1
        head = lax.slice_in_dim(cells, 0, width, axis=dim)
        tail = lax.slice_in_dim(cells, cells.shape[dim] - width, cells.shape[dim], axis=dim)
        cells = jnp.concatenate(
            [
                lax.ppermute(tail, axis, [(i, (i + 1) % count) for i in range(ends)]),
                cells,
                lax.ppermute(head, axis, [((i + 1) % count, i) for i in range(ends)]),
            ],
            axis=dim,
        )
    return cells


def lookup_dims(block_ids, block_dims):
    count = block_dims.shape[1]
    every_id = jnp.arange(count, dtype=jnp.int32)
    match = block_ids[..., None] == every_id
    rows_used = jnp.sum(jnp.where(match, block_dims[0], 0), axis=-1)
    cols_used = jnp.sum(jnp.where(match, block_dims[1], 0), axis=-1)
    return (rows_used, cols_used)


def shards(psi, left_env, right_env, term_src, block_dims):
    side = psi.shape[1]
    per_sec = left_env.shape[1]
    local_rows = psi.shape[0]
    group_size = lax.axis_size("op")
    extended = padded(psi, (("sec", 0),), local_rows)
    gathered = lax.all_gather(extended, "op", axis=0, tiled=True)
    arranged = gathered.reshape(group_size, 3, local_rows, side).transpose(1, 0, 2, 3)
    blocks = arranged.reshape(-1, side, side)
    first_block = lax.axis_index("sec") * per_sec - per_sec
    local_src = term_src - first_block
    selected = jnp.take(blocks, local_src, axis=0)
    places = jnp.arange(side, dtype=jnp.int32)
    rows_used, cols_used = lookup_dims(term_src, block_dims)
    keep = (places[:, None] < rows_used[..., None, None]) & (
        places[None, :] < cols_used[..., None, None]
    )
    masked = jnp.where(keep, selected, jnp.zeros_like(selected))
    half = jnp.einsum(
        "tkij,tkjl->tkil", masked, right_env, preferred_element_type=jnp.float32
    ).astype(jnp.bfloat16)
    partial_value = jnp.einsum("tkij,tkjl->kil", left_env, half, preferred_element_type=jnp.float32)
    partial_value = partial_value.reshape(per_sec * side, side)
    summed = lax.psum_scatter(partial_value, "op", scatter_dimension=0, tiled=True)
    row_start = (lax.axis_index("sec") * group_size + lax.axis_index("op")) * local_rows
    global_rows = row_start + jnp.arange(local_rows, dtype=jnp.int32)
    out_blocks = global_rows // side
    inner_rows = global_rows % side
    out_rows_used, out_cols_used = lookup_dims(out_blocks, block_dims)
    out_keep = (inner_rows < out_rows_used)[:, None] & (places[None, :] < out_cols_used[:, None])
    return jnp.where(out_keep, summed, jnp.zeros_like(summed)).astype(jnp.bfloat16)


def solution(mesh):
    placed = (
        P(("sec", "op"), None),
        P("op", "sec", None, None),
        P("op", "sec", None, None),
        P("op", "sec"),
        P(),
    )
    return jax.shard_map(
        shards, mesh=mesh, in_specs=placed, out_specs=P(("sec", "op"), None), check_vma=False
    )
```

profile of v0, /device:TPU:0, one launch (start us, length us, event | category | flops | bytes accessed | tf_op | source)
XLA Modules:
  0.0 178.6 jit_solution(1798577908962675282)
XLA Ops:
  6.5 0.0 all-gather.2.cloned.1.call-start
  6.5 1.3 collective-permute-start
  7.8 1.3 collective-permute-start.1
  9.1 0.0 collective-permute-done
  9.1 3.8 %collective-permute-done.1 = bf16[64,256]{1,0:T(8,128)(2,1)S(1)} collective-permute-done((bf16[64,256]{1,0:T(8,128)(2,1)}, bf16[64,256]{1,0:T(8,128)(2,1)S(1)}, u32[]{:S(2)}, u32[]{:S(2)}) %collective-permute-start.1) | collective-permute-done | bytes 32800 | tf_op jit(solution)/shard_map/ppermute | solution.py:17
  12.9 1.4 pad_maximum_fusion
  14.3 0.0 all-gather.2.cloned.1.call-update
  14.4 0.0 reduce-scatter.2.cloned.1.call-start
  14.4 0.7 compare_and_fusion
  15.1 0.1 copy.21
  15.2 0.1 reshape.72
  15.3 0.8 slice_bitcast_fusion
  16.1 1.0 select_reduce_fusion.1
  17.0 0.1 iota_compare_fusion
  17.1 45.8 %all-gather.2.cloned.1.call-done = bf16[3072,256]{1,0:T(8,128)(2,1)} async-done(((bf16[192,256]{1,0:T(8,128)(2,1)}), bf16[3072,256]{1,0:T(8,128)(2,1)}) %all-gather.2.cloned.1.call-update) | async-done | bytes 1572880 | tf_op jit(solution)/shard_map/all_gather | solution.py:39
  63.0 1.5 copy.20
  64.5 6.7 %gather_fusion = bf16[96,256,256]{2,1,0:T(8,128)(2,1)} fusion(bf16[12,256,256]{2,1,0:T(8,128)(2,1)S(1)} %bitcast.16, s32[1024]{0:T(1024)S(1)} %pad_clamp_fusion), kind=kCustom, calls=%fused_computation | custom fusion | bytes 25166208 | tf_op jit(solution)/shard_map/jit(_take)/gather | solution.py:44
  71.2 13.9 %fusion.26 = bf16[24,4,256,256]{3,2,0,1:T(8,128)(2,1)} fusion(bf16[24,4,256,256]{3,2,1,0:T(8,128)(2,1)} %param.7, bf16[24,4,256,256]{3,2,1,0:T(8,128)(2,1)} %bitcast.17, pred[24,4]{0,1:T(4,128)(4,1)S(1)} %get-tuple-element.9, pred[24,4,256]{2,0,1:T(8,128)(4,1)S(1)} %get-tuple-element.13, pred[24,4,256]{2,0,1:T(8,128)(4,1)S(1)} %get-tuple-element.14), kind=kOutput, calls=%fused_computation.7.clone.1 | convolution fusion | flops 3246391296 | bytes 37797984 | tf_op jit(solution)/shard_map/tkij,tkjl->tkil/dot_general | solution.py:51
  85.1 12.6 %fusion.1 = f32[4,256,256,1]{1,2,3,0:T(8,128)} fusion(bf16[24,4,256,256]{3,2,1,0:T(8,128)(2,1)} %param.6, bf16[24,4,256,256]{3,2,0,1:T(8,128)(2,1)} %fusion.26), kind=kOutput, calls=%fused_computation.3 | convolution fusion | flops 3221225472 | bytes 26214400 | tf_op jit(solution)/shard_map/tkij,tkjl->kil/dot_general | solution.py:54
  97.7 0.0 reduce-scatter.2.cloned.1.call-update
  97.8 0.1 select_reduce_fusion.3
  97.9 72.4 %reduce-scatter.2.cloned.1.call-done = f32[64,256]{1,0:T(8,128)} async-done(((f32[1024,256]{1,0:T(8,128)}), f32[64,256]{1,0:T(8,128)}) %reduce-scatter.2.cloned.1.call-update) | async-done | bytes 65552 | tf_op jit(solution)/shard_map/reduce_scatter | solution.py:56
  170.2 1.5 select_convert_fusion
  (3 shorter events, 0.0 us)
Async XLA Ops:
  6.5 56.4 %all-gather.2.cloned.1.call-start = ((), (), s32[]{:S(2)}) async-start(), calls=%async_computation.1 | async-start | bytes 1671168 | tf_op jit(solution)/shard_map/all_gather | solution.py:39
  6.5 2.6 %collective-permute-start = (bf16[64,256]{1,0:T(8,128)(2,1)}, bf16[64,256]{1,0:T(8,128)(2,1)S(1)}, u32[]{:S(2)}, u32[]{:S(2)}) collective-permute-start(bf16[64,256]{1,0:T(8,128)(2,1)} %param.5), channel_id=1, source_target_pairs={{0,16},{16,32},{32,48},{48,64},{64,80},{80,96},{96,112},{1,17},{17... | collective-permute-start | bytes 98312 | tf_op jit(solution)/shard_map/ppermute | solution.py:15
  7.8 5.1 %collective-permute-start.1 = (bf16[64,256]{1,0:T(8,128)(2,1)}, bf16[64,256]{1,0:T(8,128)(2,1)S(1)}, u32[]{:S(2)}, u32[]{:S(2)}) collective-permute-start(bf16[64,256]{1,0:T(8,128)(2,1)} %param.5), channel_id=1, source_target_pairs={{16,0},{32,16},{48,32},{64,48},{80,64},{96,80},{112,96},{17,1},{33... | collective-permute-start | bytes 98312 | tf_op jit(solution)/shard_map/ppermute | solution.py:17
  14.4 155.9 %reduce-scatter.2.cloned.1.call-start = ((), (), s32[]{:S(2)}) async-start(), calls=%async_computation.2 | async-start | bytes 1114112 | tf_op jit(solution)/shard_map/reduce_scatter | solution.py:56
Sparse Core Ops, SparseCore 0:
  14.5 48.4 all-gather.1
  97.8 72.3 reduce-scatter.1
where the time goes:
time: 179 us
  waiting for transfers between devices  122 us (68%)
  matrix products  26.5 us (15%)
  between operations  13.5 us (8%)
  local copies, waits for them, and re-layouts  9.17 us (5%)
  other arithmetic  4.82 us (3%)
  starting transfers between devices  2.62 us (1%)
    reduce_scatter x1, waiting for transfers between devices, shards(): lax.psum_scatter(partial_value, 'op', scatter_dimension=0, tiled=True)  72.4 us
    all_gather x1, waiting for transfers between devices, shards(): gathered = lax.all_gather(extended, 'op', axis=0, tiled=True)  45.8 us
    dot_general x1, matrix products, shards(): jnp.einsum('tkij,tkjl->tkil', masked, right_env, preferred_element_type=j...  13.9 us
    dot_general x1, matrix products, shards(): jnp.einsum('tkij,tkjl->kil', left_env, half, preferred_element_type=jnp.f...  12.6 us
    gather x1, local copies, waits for them, and re-layouts, shards(): selected = jnp.take(blocks, local_src, axis=0)  6.72 us
    ppermute x1, waiting for transfers between devices, padded(): lax.ppermute(head, axis, [((i + 1) % count, i) for i in range(ends)])  3.81 us
  transfers between devices with their start and end apart: 4, of which 3 were waited for; matrix products, arithmetic and copies ran while one was open for 2% of the time, Pallas kernels for 0%

commit v1 on v0

v1 whole, which is shorter than its diff:
```python
import functools

import jax
import jax.numpy as jnp
from jax import lax
from jax.experimental import pallas as pl
from jax.experimental.pallas import tpu as pltpu
from jax.sharding import PartitionSpec as P

MESH = pl.DeviceIdType.MESH
BF = jnp.bfloat16
F32 = jnp.float32
GROUP = 6


def keep_mask(dims, block, first_row, shape):
    rows = lax.broadcasted_iota(jnp.int32, shape, 0) + first_row
    cols = lax.broadcasted_iota(jnp.int32, shape, 1)
    return (rows < dims[0, block]) & (cols < dims[1, block])


def kernel(
    src, dims, psi, left, right, out,
    lv, rv, blocks, wide, acc, parts, got,
    env_sem, line_send, line_recv, plane_send, plane_recv, side_send, side_recv, sum_send, sum_recv,
):
    s, o = lax.axis_index("sec"), lax.axis_index("op")
    y, z = lax.div(o, 4), lax.rem(o, 4)
    terms = lv.shape[1]
    groups = terms // GROUP
    side = psi.shape[1]

    def env_copies(i, g):
        k = lax.rem(y + 1 + i, 4)
        span = pl.ds(g * GROUP, GROUP)
        return (
            pltpu.make_async_copy(left.at[span, k], lv.at[i, span], env_sem.at[0, i, g]),
            pltpu.make_async_copy(right.at[span, k], rv.at[i, span], env_sem.at[1, i, g]),
        )

    @pl.loop(0, 4)
    def _(i):
        @pl.loop(0, groups)
        def _(g):
            for copy in env_copies(i, g):
                copy.start()

    def at(row, col):
        return {"op": row * 4 + col}

    barrier = pltpu.get_barrier_semaphore()
    for d in range(1, 4):
        pl.semaphore_signal(barrier, inc=1, device_id=at(y, lax.rem(z + d, 4)), device_id_type=MESH)
        pl.semaphore_signal(barrier, inc=1, device_id=at(lax.rem(y + d, 4), z), device_id_type=MESH)

    @pl.when(s > 0)
    def _():
        pl.semaphore_signal(barrier, inc=1, device_id={"sec": s - 1}, device_id_type=MESH)

    @pl.when(s < 7)
    def _():
        pl.semaphore_signal(barrier, inc=1, device_id={"sec": s + 1}, device_id_type=MESH)

    keep = keep_mask(dims, 4 * s + y, z * 64, psi.shape)
    mine = jnp.where(keep, psi[...], jnp.zeros_like(psi))
    blocks[2 + y, z] = mine.reshape(2, 32, side)
    got[o] = jnp.zeros_like(psi)

    pl.semaphore_wait(barrier, 6 + jnp.where(s > 0, 1, 0) + jnp.where(s < 7, 1, 0))

    def send(ref, dst, send_sem, recv_sem, device):
        return pltpu.make_async_remote_copy(
            src_ref=ref, dst_ref=dst, send_sem=send_sem, recv_sem=recv_sem,
            device_id=device, device_id_type=MESH,
        )

    def line(d, h):
        ref = blocks.at[2 + y, z, h]
        device = at(y, lax.rem(z + d, 4)) if h == 0 else at(lax.rem(y + d, 4), z)
        return send(ref, ref, line_send.at[h, d - 1], line_recv.at[h], device)

    def plane(d, h):
        if h == 0:
            ref = blocks.at[2 + y, :, 0]
            device = at(lax.rem(y + d, 4), z)
        else:
            ref = blocks.at[2:6, z, 1]
            device = at(y, lax.rem(z + d, 4))
        return send(ref, ref, plane_send.at[h, d - 1], plane_recv.at[h, d - 1], device)

    def up_row(row):
        return row >= 2

    def side_row(d, action):
        row = lax.rem(y + 4 - d, 4)

        @pl.when((row >= 2) & (s < 7))
        def _():
            copy = send(
                blocks.at[2 + row, :, 0], blocks.at[row - 2, :, 0],
                side_send.at[0, d], side_recv.at[0], {"sec": s + 1},
            )
            action(copy)

        @pl.when((row < 2) & (s > 0))
        def _():
            copy = send(
                blocks.at[2 + row, :, 0], blocks.at[6 + row, :, 0],
                side_send.at[0, d], side_recv.at[1], {"sec": s - 1},
            )
            action(copy)

    def side_col(d, action):
        col = lax.rem(z + 4 - d, 4)

        @pl.when(s < 7)
        def _():
            copy = send(
                blocks.at[4:6, col, 1], blocks.at[0:2, col, 1],
                side_send.at[1, d], side_recv.at[0], {"sec": s + 1},
            )
            action(copy)

        @pl.when(s > 0)
        def _():
            copy = send(
                blocks.at[2:4, col, 1], blocks.at[6:8, col, 1],
                side_send.at[2, d], side_recv.at[1], {"sec": s - 1},
            )
            action(copy)

    start = lambda copy: copy.start()
    wait_send = lambda copy: copy.wait_send()

    for d in range(1, 4):
        line(d, 0).start()
        line(d, 1).start()

    def wait_bytes(ref, sem):
        pltpu.make_async_copy(ref, ref, sem).wait()

    wait_bytes(blocks.at[2, 0:3, 0], line_recv.at[0])
    for d in range(1, 4):
        plane(d, 0).start()
    side_row(0, start)
    wait_bytes(blocks.at[2, 0:3, 1], line_recv.at[1])
    for d in range(1, 4):
        plane(d, 1).start()
    side_col(0, start)
    for d in range(1, 4):
        plane(d, 0).wait_recv()
        side_row(d, start)
        plane(d, 1).wait_recv()
        side_col(d, start)

    @pl.when(s > 0)
    def _():
        wait_bytes(blocks.at[0:2], side_recv.at[0])

    @pl.when(s < 7)
    def _():
        wait_bytes(blocks.at[6:8], side_recv.at[1])

    base = 4 * s - 2

    def sum_copy(i, q):
        k = lax.rem(y + 1 + i, 4)
        return send(
            parts.at[i, q], got.at[o], sum_send.at[i, q], sum_recv.at[0], at(k, q)
        )

    @pl.loop(0, 4)
    def _(i):
        k = lax.rem(y + 1 + i, 4)
        acc[...] = jnp.zeros_like(acc)

        @pl.loop(0, groups)
        def _(g):
            for copy in env_copies(i, g):
                copy.wait()
            t0 = g * GROUP
            for u in range(GROUP):
                block = blocks[jnp.clip(src[k, t0 + u] - base, 0, 7)].reshape(side, side)
                wide[:, u * side : (u + 1) * side] = jnp.dot(
                    lv[i, t0 + u], block, preferred_element_type=F32
                ).astype(BF)
            tall = rv[i, pl.ds(t0, GROUP)].reshape(GROUP * side, side)
            acc[...] += jnp.dot(wide[...], tall, preferred_element_type=F32)

        parts[i] = acc[...].astype(BF).reshape(4, 64, side)
        for q in range(4):
            @pl.when((i < 3) | (q != z))
            def _():
                sum_copy(i, q).start()

    total = acc[pl.ds(pl.multiple_of(z * 64, 64), 64), :]
    wait_bytes(got.at[0:15], sum_recv.at[0])
    for j in range(16):
        total = total + got[j].astype(F32)
    out[...] = jnp.where(keep, total, jnp.zeros_like(total)).astype(BF)

    for d in range(1, 4):
        for h in range(2):
            line(d, h).wait_send()
            plane(d, h).wait_send()
    for d in range(4):
        side_row(d, wait_send)
        side_col(d, wait_send)
    for i in range(4):
        for q in range(4):
            @pl.when((i < 3) | (q != z))
            def _():
                sum_copy(i, q).wait_send()


def shards(psi, left_env, right_env, term_src, block_dims):
    terms, per_sec, side, _ = left_env.shape
    dma = pltpu.SemaphoreType.DMA
    vmem = pl.BlockSpec(memory_space=pltpu.VMEM)
    smem = pl.BlockSpec(memory_space=pltpu.SMEM)
    hbm = pl.BlockSpec(memory_space=pl.ANY)
    return pl.pallas_call(
        kernel,
        out_shape=jax.ShapeDtypeStruct(psi.shape, BF),
        in_specs=[smem, smem, vmem, hbm, hbm],
        out_specs=vmem,
        scratch_shapes=[
            pltpu.VMEM((per_sec, terms, side, side), BF),
            pltpu.VMEM((per_sec, terms, side, side), BF),
            pltpu.VMEM((8, 4, 2, 32, side), BF),
            pltpu.VMEM((side, GROUP * side), BF),
            pltpu.VMEM((side, side), F32),
            pltpu.VMEM((4, 4, 64, side), BF),
            pltpu.VMEM((16, 64, side), BF),
            dma((2, 4, terms // GROUP)),
            dma((2, 3)),
            dma((2,)),
            dma((2, 3)),
            dma((2, 3)),
            dma((3, 4)),
            dma((2,)),
            dma((4, 4)),
            dma((1,)),
        ],
        compiler_params=pltpu.CompilerParams(
            collective_id=0, has_side_effects=True, vmem_limit_bytes=48 * 2**20
        ),
    )(term_src.T, block_dims, psi, left_env, right_env)


def solution(mesh):
    placed = (
        P(("sec", "op"), None),
        P("op", "sec", None, None),
        P("op", "sec", None, None),
        P("op", "sec"),
        P(),
    )
    return jax.shard_map(
        shards, mesh=mesh, in_specs=placed, out_specs=P(("sec", "op"), None), check_vma=False
    )
```

time: 179 us -> 37.9 us (0.21)
  the two profiles are of different devices: /device:TPU:0 before, /device:TPU:1 now
where the time goes in v1:
time: 37.9 us; the launch traced here: 37.7 us
  Pallas kernels  34.9 us (92%)
  local copies, waits for them, and re-layouts  2.73 us (7%)
    pallas_call x1, Pallas kernels, shards(): pl.pallas_call(kernel, out_shape=jax.ShapeDtypeStruct(psi.shape, BF), in_...  34.9 us
    unnamed x7, local copies, waits for them, and re-layouts  2.73 us

profile of v1, /device:TPU:1, one launch (start us, length us, event | category | flops | bytes accessed | tf_op | source)
XLA Modules:
  0.0 37.7 jit_solution(6879476359372000702)
XLA Ops:
  0.0 0.0 copy-start
  0.0 0.8 %copy-done = bf16[64,256]{1,0:T(8,128)(2,1)S(1)} copy-done((bf16[64,256]{1,0:T(8,128)(2,1)S(1)}, bf16[64,256]{1,0:T(8,128)(2,1)}, u32[]{:S(2)}) %copy-start) | copy-done | bytes 32792
  0.8 0.0 copy-start.1
  0.8 0.7 %copy-done.1 = s32[24,4]{0,1:T(4,128)S(1)} copy-done((s32[24,4]{0,1:T(4,128)S(1)}, s32[24,4]{0,1:T(4,128)}, u32[]{:S(2)}) %copy-start.1) | copy-done | bytes 408
  1.4 0.0 copy-start.2
  1.4 0.7 %copy-done.2 = s32[2,32]{1,0:T(2,128)S(1)} copy-done((s32[2,32]{1,0:T(2,128)S(1)}, s32[2,32]{1,0:T(2,128)}, u32[]{:S(2)}) %copy-start.2) | copy-done | bytes 280
  2.1 34.9 %shard_map.55 = bf16[64,256]{1,0:T(8,128)(2,1)S(1)} custom-call(s32[4,24]{1,0:T(4,128)S(1)} %bitcast.1, s32[2,32]{1,0:T(2,128)S(1)} %copy-done.2, bf16[64,256]{1,0:T(8,128)(2,1)S(1)} %copy-done, bf16[24,4,256,256]{3,2,1,0:T(8,128)(2,1)} %left.1, bf16[24,4,256,256]{3,2,1,0:T(8,128)(2,1)} %right.1), custom_call_target="tpu_custom_call" | custom-call | tf_op jit(solution)/shard_map/pallas_call | solution.py:222
  37.1 0.6 %copy.7 = bf16[64,256]{1,0:T(8,128)(2,1)} copy(bf16[64,256]{1,0:T(8,128)(2,1)S(1)} %shard_map.55) | data formatting | bytes 65536
Async XLA Ops:
  0.0 0.8 %copy-start = (bf16[64,256]{1,0:T(8,128)(2,1)S(1)}, bf16[64,256]{1,0:T(8,128)(2,1)}, u32[]{:S(2)}) copy-start(bf16[64,256]{1,0:T(8,128)(2,1)} %psi.1) | copy-start | bytes 98308
  0.8 0.7 %copy-start.1 = (s32[24,4]{0,1:T(4,128)S(1)}, s32[24,4]{0,1:T(4,128)}, u32[]{:S(2)}) copy-start(s32[24,4]{0,1:T(4,128)} %param.8) | copy-start | bytes 1156
  1.4 0.7 %copy-start.2 = (s32[2,32]{1,0:T(2,128)S(1)}, s32[2,32]{1,0:T(2,128)}, u32[]{:S(2)}) copy-start(s32[2,32]{1,0:T(2,128)} %dims.1) | copy-start | bytes 772

commit v2 on v0

v2 whole, which is shorter than its diff:
```python
import jax
import jax.numpy as jnp
from jax import lax
from jax.experimental import pallas as pl
from jax.experimental.pallas import tpu as pltpu
from jax.sharding import PartitionSpec as P

MESH = pl.DeviceIdType.MESH
BF = jnp.bfloat16
F32 = jnp.float32
GROUP = 6
OFFSETS = sorted(
    [(a, b) for a in range(4) for b in range(4) if a or b],
    key=lambda p: min(p[0], 4 - p[0]) + min(p[1], 4 - p[1]),
)


def keep_mask(dims, block, first_row, shape):
    rows = lax.broadcasted_iota(jnp.int32, shape, 0) + first_row
    cols = lax.broadcasted_iota(jnp.int32, shape, 1)
    return (rows < dims[0, block]) & (cols < dims[1, block])


def kernel(
    src_hbm, dims_hbm, psi_hbm, left, right, out,
    src, dims, psi, lv, rv, blocks, across, wide, acc, parts, got,
    small_sem, env_sem, plane_send, plane_recv, side_send, chip_recv, across_recv, sum_send, sum_recv,
):
    s, o = lax.axis_index("sec"), lax.axis_index("op")
    y, z = lax.div(o, 4), lax.rem(o, 4)
    core = lax.rem(s, 2)
    terms = lv.shape[1]
    groups = terms // GROUP
    side = psi.shape[1]

    small = [
        pltpu.make_async_copy(psi_hbm, psi, small_sem.at[0]),
        pltpu.make_async_copy(dims_hbm, dims, small_sem.at[1]),
        pltpu.make_async_copy(src_hbm, src, small_sem.at[2]),
    ]
    for copy in small:
        copy.start()

    odd = lax.rem(y, 2)
    first = 2 - 2 * core
    last = 2 * core
    order = [first + odd, first + 1 - odd, last + 1 - odd, last + odd]

    def env_copies(i, g):
        span = pl.ds(g * GROUP, GROUP)
        return (
            pltpu.make_async_copy(left.at[span, order[i]], lv.at[i, span], env_sem.at[0, i, g]),
            pltpu.make_async_copy(right.at[span, order[i]], rv.at[i, span], env_sem.at[1, i, g]),
        )

    def peer(d):
        return {"op": lax.rem(y + OFFSETS[d][0], 4) * 4 + lax.rem(z + OFFSETS[d][1], 4)}

    barrier = pltpu.get_barrier_semaphore()
    for d in range(15):
        pl.semaphore_signal(barrier, inc=1, device_id=peer(d), device_id_type=MESH)

    @pl.when(s > 0)
    def _():
        pl.semaphore_signal(barrier, inc=1, device_id={"sec": s - 1}, device_id_type=MESH)

    @pl.when(s < 7)
    def _():
        pl.semaphore_signal(barrier, inc=1, device_id={"sec": s + 1}, device_id_type=MESH)

    for i in range(4):
        for g in range(groups):
            for copy in env_copies(i, g):
                copy.start()

    small[0].wait()
    small[1].wait()
    keep = keep_mask(dims, 4 * s + y, z * 64, psi.shape)
    mine = psi[...]
    blocks[2 + y, z] = jnp.where(keep, mine, jnp.zeros_like(mine))
    got[o] = jnp.zeros_like(mine)

    pl.semaphore_wait(barrier, 15 + jnp.where(s > 0, 1, 0) + jnp.where(s < 7, 1, 0))

    def send(ref, dst, send_sem, recv_sem, device):
        return pltpu.make_async_remote_copy(
            src_ref=ref, dst_ref=dst, send_sem=send_sem, recv_sem=recv_sem,
            device_id=device, device_id_type=MESH,
        )

    def wait_bytes(ref, sem):
        pltpu.make_async_copy(ref, ref, sem).wait()

    def plane(d):
        ref = blocks.at[2 + y, z]
        return send(ref, ref, plane_send.at[d], plane_recv.at[d], peer(d))

    def forward(n, row, col, action):
        up = row >= 2
        to = s + jnp.where(up, 1, -1)
        on_chip = up == (core == 0)

        @pl.when(on_chip)
        def _():
            place = jnp.where(up, row - 2, row + 6)
            action(
                send(blocks.at[2 + row, col], blocks.at[place, col], side_send.at[n], chip_recv.at[0], {"sec": to})
            )

        @pl.when(jnp.logical_not(on_chip) & (to >= 0) & (to <= 7))
        def _():
            action(
                send(
                    blocks.at[2 + row, col], across.at[lax.rem(row, 2), col],
                    side_send.at[n], across_recv.at[0], {"sec": to},
                )
            )

    def forward_from(d, action):
        row, col = OFFSETS[d]
        forward(d, lax.rem(y + 4 - row, 4), lax.rem(z + 4 - col, 4), action)

    start = lambda copy: copy.start()
    wait_send = lambda copy: copy.wait_send()

    forward(15, y, z, start)
    for d in range(15):
        plane(d).start()
    for d in range(15):
        plane(d).wait_recv()
        forward_from(d, start)
    wait_bytes(blocks.at[0:2], chip_recv.at[0])
    small[2].wait()
    for i in range(4):
        for g in range(groups):
            for copy in env_copies(i, g):
                copy.wait()

    base = 4 * s - 2

    def sum_copy(i, q):
        return send(parts.at[i, q], got.at[o], sum_send.at[i, q], sum_recv.at[0], {"op": 4 * order[i] + q})

    def each_sum(i, action):
        for q in range(4):
            if i in (1, 2):
                action(sum_copy(i, q))
            else:
                @pl.when(4 * order[i] + q != o)
                def _():
                    action(sum_copy(i, q))

    for i in range(4):
        k = order[i]
        if i == 2:
            inside = jnp.where(core == 0, s > 0, s < 7)

            @pl.when(inside)
            def _():
                wait_bytes(across, across_recv.at[0])
                blocks[pl.ds(6 * core, 2)] = across[...]

        for g in range(groups):
            t0 = g * GROUP
            for u in range(GROUP):
                block = blocks[jnp.clip(src[k, t0 + u] - base, 0, 7)].reshape(side, side)
                wide[g % 2, :, u * side : (u + 1) * side] = jnp.dot(
                    lv[i, t0 + u], block, preferred_element_type=F32
                ).astype(BF)
            tall = rv[i, t0 : t0 + GROUP].reshape(GROUP * side, side)
            part = jnp.dot(wide[g % 2], tall, preferred_element_type=F32)
            if g == 0:
                acc[i] = part
            else:
                acc[i] += part

        parts[i] = acc[i].astype(BF).reshape(4, 64, side)
        each_sum(i, start)

    own = jnp.where((y >= 2) == (core == 1), 3, 0)
    total = acc[own, pl.ds(pl.multiple_of(z * 64, 64), 64), :]
    wait_bytes(got.at[0:15], sum_recv.at[0])
    for j in range(16):
        total = total + got[j].astype(F32)
    out[...] = jnp.where(keep, total, jnp.zeros_like(total)).astype(BF)

    for d in range(15):
        plane(d).wait_send()
        forward_from(d, wait_send)
    forward(15, y, z, wait_send)
    for i in range(4):
        each_sum(i, wait_send)


def shards(psi, left_env, right_env, term_src, block_dims):
    terms, per_sec, side, _ = left_env.shape
    rows = psi.shape[0]
    dma = pltpu.SemaphoreType.DMA
    return pl.pallas_call(
        kernel,
        out_shape=jax.ShapeDtypeStruct(psi.shape, BF),
        in_specs=[pl.BlockSpec(memory_space=pl.ANY)] * 5,
        out_specs=pl.BlockSpec(memory_space=pltpu.VMEM),
        scratch_shapes=[
            pltpu.SMEM((per_sec, terms), jnp.int32),
            pltpu.SMEM(block_dims.shape, jnp.int32),
            pltpu.VMEM(psi.shape, BF),
            pltpu.VMEM((per_sec, terms, side, side), BF),
            pltpu.VMEM((per_sec, terms, side, side), BF),
            pltpu.VMEM((8, 4, rows, side), BF),
            pltpu.VMEM((2, 4, rows, side), BF),
            pltpu.VMEM((2, side, GROUP * side), BF),
            pltpu.VMEM((4, side, side), F32),
            pltpu.VMEM((4, 4, rows, side), BF),
            pltpu.VMEM((16, rows, side), BF),
            dma((3,)),
            dma((2, 4, terms // GROUP)),
            dma((15,)),
            dma((15,)),
            dma((16,)),
            dma((1,)),
            dma((1,)),
            dma((4, 4)),
            dma((1,)),
        ],
        compiler_params=pltpu.CompilerParams(
            collective_id=0, has_side_effects=True, vmem_limit_bytes=48 * 2**20
        ),
    )(*[pltpu.with_memory_space_constraint(a, pltpu.HBM) for a in (term_src.T, block_dims, psi, left_env, right_env)])


def solution(mesh):
    placed = (
        P(("sec", "op"), None),
        P("op", "sec", None, None),
        P("op", "sec", None, None),
        P("op", "sec"),
        P(),
    )
    return jax.shard_map(
        shards, mesh=mesh, in_specs=placed, out_specs=P(("sec", "op"), None), check_vma=False
    )
```

time: 179 us -> 30.5 us (0.17)
  waiting for transfers between devices: 122 us -> 0 us
  Pallas kernels: 0 us -> 29.8 us
  matrix products: 26.5 us -> 0 us
  between operations: 13.5 us -> 0.01 us
  local copies, waits for them, and re-layouts: 9.17 us -> 0.62 us
  other arithmetic: 4.82 us -> 0 us
  starting transfers between devices: 2.62 us -> 0 us
    reduce_scatter x1 -> x0, waiting for transfers between devices: 72.4 us -> none  [shards(): lax.psum_scatter(partial_value, 'op', scatter_dimension=0, tiled=True)]
    all_gather x1 -> x0, waiting for transfers between devices: 45.8 us -> none  [shards(): gathered = lax.all_gather(extended, 'op', axis=0, tiled=True)]
    pallas_call x0 -> x1, Pallas kernels: none -> 29.8 us  [shards(): pl.pallas_call(kernel, out_shape=jax.ShapeDtypeStruct(psi.shape, BF), in_...]
    dot_general x2 -> x0, matrix products: 26.5 us -> none  [the longest x1 13.9 us: shards(): jnp.einsum('tkij,tkjl->tkil', masked, right_env, preferred_element_type=j...]
    gather x1 -> x0, local copies, waits for them, and re-layouts: 6.72 us -> none  [shards(): selected = jnp.take(blocks, local_src, axis=0)]
    ppermute x2 -> x0, waiting for transfers between devices: 3.81 us -> none  [the longest x1 3.81 us: padded(): lax.ppermute(head, axis, [((i + 1) % count, i) for i in range(ends)])]
    ppermute x2 -> x0, starting transfers between devices: 2.57 us -> none  [the longest x1 1.29 us: padded(): lax.ppermute(head, axis, [((i + 1) % count, i) for i in range(ends)])]
  transfers between devices with their start and end apart: 4 -> 0, of which waited for: 3 -> 0; matrix products, arithmetic and copies ran while one was open for 2% -> 0% of each run, Pallas kernels for 0% -> 0%
where the time goes in v2:
time: 30.5 us; the launch traced here: 30.4 us
  Pallas kernels  29.8 us (98%)
  local copies, waits for them, and re-layouts  0.62 us (2%)
    pallas_call x1, Pallas kernels, shards(): pl.pallas_call(kernel, out_shape=jax.ShapeDtypeStruct(psi.shape, BF), in_...  29.8 us
    unnamed x1, local copies, waits for them, and re-layouts  0.62 us

profile of v2, /device:TPU:0, one launch (start us, length us, event | category | flops | bytes accessed | tf_op | source)
XLA Modules:
  0.0 30.4 jit_solution(11455564499741093742)
XLA Ops:
  0.0 29.8 %shard_map.55 = bf16[64,256]{1,0:T(8,128)(2,1)S(1)} custom-call(s32[4,24]{1,0:T(4,128)} %bitcast.1, s32[2,32]{1,0:T(2,128)} %dims_hbm.1, bf16[64,256]{1,0:T(8,128)(2,1)} %psi_hbm.1, bf16[24,4,256,256]{3,2,1,0:T(8,128)(2,1)} %left.1, bf16[24,4,256,256]{3,2,1,0:T(8,128)(2,1)} %right.1), custom_call_target="tpu_custom_call" | custom-call | tf_op jit(solution)/shard_map/pallas_call | solution.py:199
  29.8 0.6 %copy.7 = bf16[64,256]{1,0:T(8,128)(2,1)} copy(bf16[64,256]{1,0:T(8,128)(2,1)S(1)} %shard_map.55) | data formatting | bytes 65536

commit v3 on v2

--- a/solution.py
+++ b/solution.py
@@ -11,7 +11,7 @@
 GROUP = 6
 OFFSETS = sorted(
     [(a, b) for a in range(4) for b in range(4) if a or b],
-    key=lambda p: min(p[0], 4 - p[0]) + min(p[1], 4 - p[1]),
+    key=lambda p: (min(p[0], 4 - p[0]) + min(p[1], 4 - p[1]), p[1] != 0),
 )
 
 
@@ -42,22 +42,22 @@
         copy.start()
 
     odd = lax.rem(y, 2)
-    first = 2 - 2 * core
-    last = 2 * core
-    order = [first + odd, first + 1 - odd, last + 1 - odd, last + odd]
-
-    def env_copies(i, g):
-        span = pl.ds(g * GROUP, GROUP)
+    near = 2 - 2 * core
+    far = 2 * core
+    end = jnp.where((y >= 2) == (core == 1), y, 3 - y)
+    order = [near + odd, near + 1 - odd, 4 * core + 1 - end, end]
+
+    def env_copies(i):
         return (
-            pltpu.make_async_copy(left.at[span, order[i]], lv.at[i, span], env_sem.at[0, i, g]),
-            pltpu.make_async_copy(right.at[span, order[i]], rv.at[i, span], env_sem.at[1, i, g]),
+            pltpu.make_async_copy(left.at[:, order[i]], lv.at[i], env_sem.at[0, i]),
+            pltpu.make_async_copy(right.at[:, order[i]], rv.at[i], env_sem.at[1, i]),
         )
 
     def peer(d):
         return {"op": lax.rem(y + OFFSETS[d][0], 4) * 4 + lax.rem(z + OFFSETS[d][1], 4)}
 
     barrier = pltpu.get_barrier_semaphore()
-    for d in range(15):
+    for d in reversed(range(15)):
         pl.semaphore_signal(barrier, inc=1, device_id=peer(d), device_id_type=MESH)
 
     @pl.when(s > 0)
@@ -67,11 +67,6 @@
     @pl.when(s < 7)
     def _():
         pl.semaphore_signal(barrier, inc=1, device_id={"sec": s + 1}, device_id_type=MESH)
-
-    for i in range(4):
-        for g in range(groups):
-            for copy in env_copies(i, g):
-                copy.start()
 
     small[0].wait()
     small[1].wait()
@@ -93,56 +88,63 @@
 
     def plane(d):
         ref = blocks.at[2 + y, z]
-        return send(ref, ref, plane_send.at[d], plane_recv.at[d], peer(d))
-
-    def forward(n, row, col, action):
-        up = row >= 2
-        to = s + jnp.where(up, 1, -1)
-        on_chip = up == (core == 0)
-
-        @pl.when(on_chip)
-        def _():
-            place = jnp.where(up, row - 2, row + 6)
-            action(
-                send(blocks.at[2 + row, col], blocks.at[place, col], side_send.at[n], chip_recv.at[0], {"sec": to})
-            )
-
-        @pl.when(jnp.logical_not(on_chip) & (to >= 0) & (to <= 7))
+        return send(ref, ref, plane_send.at[d], plane_recv.at[o], peer(d))
+
+    def arrived(row, col):
+        wait_bytes(blocks.at[2 + row, col], plane_recv.at[4 * row + col])
+
+    waits = (y >= 2) == (core == 1)
+    sibling = s + 1 - 2 * core
+    beyond = s - 1 + 2 * core
+
+    def slabs(pair):
+        return [(pair + a, lax.rem(z + b, 4), 4 * a + b) for a in range(2) for b in range(4)]
+
+    def to_sibling(row, col, n, action):
+        place = row - 2 + 8 * core
+        action(send(blocks.at[2 + row, col], blocks.at[place, col], side_send.at[n], chip_recv.at[0], {"sec": sibling}))
+
+    def to_beyond(row, col, n, action):
+        @pl.when((beyond >= 0) & (beyond <= 7))
         def _():
             action(
                 send(
                     blocks.at[2 + row, col], across.at[lax.rem(row, 2), col],
-                    side_send.at[n], across_recv.at[0], {"sec": to},
+                    side_send.at[8 + n], across_recv.at[0], {"sec": beyond},
                 )
             )
 
-    def forward_from(d, action):
-        row, col = OFFSETS[d]
-        forward(d, lax.rem(y + 4 - row, 4), lax.rem(z + 4 - col, 4), action)
-
     start = lambda copy: copy.start()
     wait_send = lambda copy: copy.wait_send()
 
-    forward(15, y, z, start)
-    for d in range(15):
+    for d in reversed(range(15)):
         plane(d).start()
-    for d in range(15):
-        plane(d).wait_recv()
-        forward_from(d, start)
+    for i in range(4):
+        for copy in env_copies(i):
+            copy.start()
+    for row, col, n in slabs(near):
+        @pl.when(((row != y) | (col != z)))
+        def _():
+            arrived(row, col)
+        to_sibling(row, col, n, start)
+    for row, col, n in slabs(far):
+        @pl.when((row != y) | (col != z))
+        def _():
+            arrived(row, col)
+        to_beyond(row, col, n, start)
     wait_bytes(blocks.at[0:2], chip_recv.at[0])
     small[2].wait()
     for i in range(4):
-        for g in range(groups):
-            for copy in env_copies(i, g):
-                copy.wait()
+        for copy in env_copies(i):
+            copy.wait()
 
     base = 4 * s - 2
 
     def sum_copy(i, q):
         return send(parts.at[i, q], got.at[o], sum_send.at[i, q], sum_recv.at[0], {"op": 4 * order[i] + q})
 
-    def each_sum(i, action):
-        for q in range(4):
+    def each_sum(i, quarters, action):
+        for q in quarters:
             if i in (1, 2):
                 action(sum_copy(i, q))
             else:
@@ -160,22 +162,32 @@
                 wait_bytes(across, across_recv.at[0])
                 blocks[pl.ds(6 * core, 2)] = across[...]
 
-        for g in range(groups):
-            t0 = g * GROUP
-            for u in range(GROUP):
-                block = blocks[jnp.clip(src[k, t0 + u] - base, 0, 7)].reshape(side, side)
-                wide[g % 2, :, u * side : (u + 1) * side] = jnp.dot(
-                    lv[i, t0 + u], block, preferred_element_type=F32
-                ).astype(BF)
-            tall = rv[i, t0 : t0 + GROUP].reshape(GROUP * side, side)
-            part = jnp.dot(wide[g % 2], tall, preferred_element_type=F32)
-            if g == 0:
-                acc[i] = part
-            else:
-                acc[i] += part
-
-        parts[i] = acc[i].astype(BF).reshape(4, 64, side)
-        each_sum(i, start)
+        for lo, hi in ((0, side),) if i < 3 else ((0, side // 2), (side // 2, side)):
+            for g in range(groups):
+                t0 = g * GROUP
+                for u in range(GROUP):
+                    block = blocks[jnp.clip(src[k, t0 + u] - base, 0, 7)].reshape(side, side)
+                    wide[g % 2, lo:hi, u * side : (u + 1) * side] = jnp.dot(
+                        lv[i, t0 + u, lo:hi], block, preferred_element_type=F32
+                    ).astype(BF)
+                tall = rv[i, t0 : t0 + GROUP].reshape(GROUP * side, side)
+                part = jnp.dot(wide[g % 2, lo:hi], tall, preferred_element_type=F32)
+                if g == 0:
+                    acc[i, lo:hi] = part
+                else:
+                    acc[i, lo:hi] += part
+
+            parts[i, lo // 64 : hi // 64] = acc[i, lo:hi].astype(BF).reshape((hi - lo) // 64, 64, side)
+            each_sum(i, range(lo // 64, hi // 64), start)
+
+    for d in range(15):
+        plane(d).wait_send()
+    for row, col, n in slabs(near):
+        to_sibling(row, col, n, wait_send)
+    for row, col, n in slabs(far):
+        to_beyond(row, col, n, wait_send)
+    for i in range(4):
+        each_sum(i, range(4), wait_send)
 
     own = jnp.where((y >= 2) == (core == 1), 3, 0)
     total = acc[own, pl.ds(pl.multiple_of(z * 64, 64), 64), :]
@@ -183,13 +195,6 @@
     for j in range(16):
         total = total + got[j].astype(F32)
     out[...] = jnp.where(keep, total, jnp.zeros_like(total)).astype(BF)
-
-    for d in range(15):
-        plane(d).wait_send()
-        forward_from(d, wait_send)
-    forward(15, y, z, wait_send)
-    for i in range(4):
-        each_sum(i, wait_send)
 
 
 def shards(psi, left_env, right_env, term_src, block_dims):
@@ -214,9 +219,9 @@
             pltpu.VMEM((4, 4, rows, side), BF),
             pltpu.VMEM((16, rows, side), BF),
             dma((3,)),
-            dma((2, 4, terms // GROUP)),
+            dma((2, 4)),
             dma((15,)),
-            dma((15,)),
+            dma((16,)),
             dma((16,)),
             dma((1,)),
             dma((1,)),

time: 30.5 us -> 28.4 us (0.931)
  Pallas kernels: 29.8 us -> 27.4 us
    pallas_call x1, Pallas kernels: 29.8 us -> 27.4 us  [shards(): pl.pallas_call(kernel, out_shape=jax.ShapeDtypeStruct(psi.shape, BF), in_...]
where the time goes in v3:
time: 28.4 us; the launch traced here: 28.1 us
  Pallas kernels  27.4 us (96%)
  local copies, waits for them, and re-layouts  0.62 us (2%)
    pallas_call x1, Pallas kernels, shards(): pl.pallas_call(kernel, out_shape=jax.ShapeDtypeStruct(psi.shape, BF), in_...  27.4 us
    unnamed x1, local copies, waits for them, and re-layouts  0.62 us

profile of v3, /device:TPU:0, one launch (start us, length us, event | category | flops | bytes accessed | tf_op | source)
XLA Modules:
  0.0 28.1 jit_solution(11653205144733743128)
XLA Ops:
  0.0 27.4 %shard_map.55 = bf16[64,256]{1,0:T(8,128)(2,1)S(1)} custom-call(s32[4,24]{1,0:T(4,128)} %bitcast.1, s32[2,32]{1,0:T(2,128)} %dims_hbm.1, bf16[64,256]{1,0:T(8,128)(2,1)} %psi_hbm.1, bf16[24,4,256,256]{3,2,1,0:T(8,128)(2,1)} %left.1, bf16[24,4,256,256]{3,2,1,0:T(8,128)(2,1)} %right.1), custom_call_target="tpu_custom_call" | custom-call | tf_op jit(solution)/shard_map/pallas_call | solution.py:204
  27.4 0.6 %copy.7 = bf16[64,256]{1,0:T(8,128)(2,1)} copy(bf16[64,256]{1,0:T(8,128)(2,1)S(1)} %shard_map.55) | data formatting | bytes 65536

commit v4 on v3

--- a/solution.py
+++ b/solution.py
@@ -75,6 +75,9 @@
     blocks[2 + y, z] = jnp.where(keep, mine, jnp.zeros_like(mine))
     got[o] = jnp.zeros_like(mine)
 
+    for i in range(4):
+        for copy in env_copies(i):
+            copy.start()
     pl.semaphore_wait(barrier, 15 + jnp.where(s > 0, 1, 0) + jnp.where(s < 7, 1, 0))
 
     def send(ref, dst, send_sem, recv_sem, device):
@@ -119,9 +122,6 @@
 
     for d in reversed(range(15)):
         plane(d).start()
-    for i in range(4):
-        for copy in env_copies(i):
-            copy.start()
     for row, col, n in slabs(near):
         @pl.when(((row != y) | (col != z)))
         def _():

time: 28.4 us -> 28.2 us (level)
  no operation moved by 1% of the time
where the time goes in v4:
time: 28.2 us; the launch traced here: 28 us
  Pallas kernels  27.4 us (97%)
  local copies, waits for them, and re-layouts  0.62 us (2%)
    pallas_call x1, Pallas kernels, shards(): pl.pallas_call(kernel, out_shape=jax.ShapeDtypeStruct(psi.shape, BF), in_...  27.4 us
    unnamed x1, local copies, waits for them, and re-layouts  0.62 us

profile of v4, /device:TPU:0, one launch (start us, length us, event | category | flops | bytes accessed | tf_op | source)
XLA Modules:
  0.0 28.0 jit_solution(8815731111424912720)
XLA Ops:
  0.0 27.4 %shard_map.55 = bf16[64,256]{1,0:T(8,128)(2,1)S(1)} custom-call(s32[4,24]{1,0:T(4,128)} %bitcast.1, s32[2,32]{1,0:T(2,128)} %dims_hbm.1, bf16[64,256]{1,0:T(8,128)(2,1)} %psi_hbm.1, bf16[24,4,256,256]{3,2,1,0:T(8,128)(2,1)} %left.1, bf16[24,4,256,256]{3,2,1,0:T(8,128)(2,1)} %right.1), custom_call_target="tpu_custom_call" | custom-call | tf_op jit(solution)/shard_map/pallas_call | solution.py:204
  27.4 0.6 %copy.7 = bf16[64,256]{1,0:T(8,128)(2,1)} copy(bf16[64,256]{1,0:T(8,128)(2,1)S(1)} %shard_map.55) | data formatting | bytes 65536
